TPU v7x, 256 devices: a whole 4x4x8 slice. The times are simulated.
256 devices in a mesh: row: 32 (over y_hi, z, core), rep: 8 (over x, y_lo).
Axes of the slice: x: 4, y: 4 (y_hi: 2, y_lo: 2; y = y_hi * 2 + y_lo), z: 8, core: 2. Of those that a mesh axis runs over, the one named last changes fastest.
Arguments:
- features: bfloat16 [65536, 256], P(('row', 'rep')), may hold values from -6 to 6
- tiles: bfloat16 [16384, 256, 256], P(('row', 'rep')), may hold values from -0.078125 to 0.078125
- tile_target: int32 [256, 64], P(('row', 'rep')), may hold values from 0 to 7
- tile_count: int32 [256, 32], P(('row', 'rep')), may hold values from 0 to 2, as said below
- weight: bfloat16 [256, 256], replicated, may hold values from -0.375 to 0.375
- cotangent: bfloat16 [65536, 256], P(('row', 'rep')), may hold values from -6 to 6
Outputs:
- hidden_out: bfloat16 [65536, 256], P(('row', 'rep'))
- feature_grad: bfloat16 [65536, 256], P(('row', 'rep'))
- weight_grad: float32 [256, 256], replicated
Inputs may be any that keep to these rules, and one draw needn't show every extreme that they name: Slot j of source partition c is live exactly when j < tile_count; in every draw some block list has all 2 slots of every source partition live. `tile_target`: read only where the slot is live.
All inputs are finite; a program needn't handle non-finite values.
Results may differ from a plain program's by a relative error of at most 0.027.
Values may be sent and summed in bfloat16 or wider, within the bound.
A program may use at most 128 MiB of HBM per device.

v0:
```python
import jax
import jax.numpy as jnp
from jax import lax
from jax.sharding import PartitionSpec as P


def slot_window(tiles, select, blocks, slot_count, tile_rows, rep_count):
    return (
        tiles.reshape(blocks, slot_count, tile_rows, tile_rows),
        select.reshape(blocks, slot_count, rep_count),
    )


def local(features, tiles, tile_target, tile_count, weight, cotangent):
    tile_rows, width = features.shape
    row_count = lax.axis_size("row")
    rep_count = lax.axis_size("rep")
    slot_count = tiles.shape[0] // row_count
    slot_index = jnp.arange(slot_count, dtype=jnp.int32)
    live = slot_index[None, :] < tile_count[0][:, None]
    targets = tile_target[0].reshape(row_count, slot_count)
    select = (
        jax.nn.one_hot(targets, rep_count, dtype=jnp.float32) * live[:, :, None].astype(jnp.float32)
    ).reshape(row_count * slot_count, rep_count)
    select_half = select.astype(jnp.bfloat16)
    portion = lax.all_gather(features, "row", axis=0, tiled=True)
    blocks = portion.shape[0] // tile_rows
    tile_part, select_part = slot_window(tiles, select, blocks, slot_count, tile_rows, rep_count)
    source_rows = portion.reshape(blocks, tile_rows, width)
    products = jnp.einsum(
        "bjtu,buf->bjtf", tile_part, source_rows, preferred_element_type=jnp.float32
    )
    added = jnp.einsum("bjq,bjtf->qtf", select_part, products, precision=lax.Precision.HIGHEST)
    partial_value = added.reshape(rep_count * tile_rows, width)
    aggregate = lax.psum_scatter(
        partial_value.astype(jnp.bfloat16), "rep", scatter_dimension=0, tiled=True
    )
    pre = jnp.dot(aggregate, weight, preferred_element_type=jnp.float32)
    sigma = jax.nn.sigmoid(pre)
    hidden_out = (pre * sigma).astype(jnp.bfloat16)
    grad_pre = (cotangent.astype(jnp.float32) * sigma * (1.0 + pre * (1.0 - sigma))).astype(
        jnp.bfloat16
    )
    weight_term = jnp.einsum("tf,tg->fg", aggregate, grad_pre, preferred_element_type=jnp.float32)
    dagg = jnp.einsum("tg,fg->tf", grad_pre, weight, preferred_element_type=jnp.float32).astype(
        jnp.bfloat16
    )
    dagg_full = lax.all_gather(dagg, "rep", axis=0, tiled=True)
    weight_grad = lax.psum(weight_term, ("row", "rep"))
    dagg_blocks = dagg_full.reshape(rep_count, tile_rows, width)
    count = lax.axis_size("row") * tile_rows
    blocks = count // tile_rows
    tile_part, select_part = slot_window(
        tiles, select_half, blocks, slot_count, tile_rows, rep_count
    )
    picked = jnp.einsum(
        "bjq,qtf->bjtf", select_part, dagg_blocks, preferred_element_type=jnp.float32
    ).astype(jnp.bfloat16)
    result = jnp.einsum("bjtu,bjtf->buf", tile_part, picked, preferred_element_type=jnp.float32)
    feature_grad = lax.psum_scatter(
        result.reshape(count, width).astype(jnp.bfloat16), "row", scatter_dimension=0, tiled=True
    )
    return (hidden_out, feature_grad, weight_grad)


def solution(mesh):
    return jax.shard_map(
        local,
        mesh=mesh,
        in_specs=(
            P(("row", "rep"), None),
            P(("row", "rep"), None, None),
            P(("row", "rep"), None),
            P(("row", "rep"), None),
            P(),
            P(("row", "rep"), None),
        ),
        out_specs=(P(("row", "rep"), None), P(("row", "rep"), None), P()),
        check_vma=False,
    )
```

profile of v0, /device:TPU:2, one launch (start us, length us, event | category | flops | bytes accessed | tf_op | source)
XLA Modules:
  0.0 614.6 jit_solution(7869653896773148963)
XLA Ops:
  7.2 0.0 copy-start
  7.2 0.0 all-gather.3.cloned.1.call-start
  7.2 0.7 all-gather.3.cloned.1.call-update
  7.9 0.0 reduce-scatter.3.cloned.1.call-start
  8.0 0.5 broadcast.90
  8.5 1.3 reduce.3
  9.8 0.1 eq.43
  9.9 0.1 copy.12
  10.0 0.7 compare_convert_fusion
  10.6 90.0 %all-gather.3.cloned.1.call-done = bf16[8192,256]{1,0:T(8,128)(2,1)} async-done(((bf16[256,256]{1,0:T(8,128)(2,1)}), bf16[8192,256]{1,0:T(8,128)(2,1)}) %all-gather.3.cloned.1.call-update) | async-done | bytes 4194320 | tf_op jit(solution)/shard_map/all_gather | solution.py:26
  100.6 12.7 %fusion.19 = f32[32,2,256,256]{3,2,1,0:T(8,128)} fusion(bf16[32,2,256,256]{3,2,1,0:T(8,128)(2,1)} %bitcast.38, bf16[32,256,256,1]{2,1,3,0:T(8,128)(2,1)} %bitcast.40), kind=kOutput, calls=%fused_computation.27 | convolution fusion | flops 2147483648 | bytes 29360128 | tf_op jit(solution)/shard_map/bjtu,buf->bjtf/dot_general | solution.py:30
  113.3 0.0 copy-start.1
  113.3 22.6 %bitcast_convert_fusion.1 = bf16[8,256,256]{2,0,1:T(8,128)(2,1)S(1)} fusion(f32[32,2,256,256]{3,2,1,0:T(8,128)} %fusion.19, f32[32,2]{0,1:T(2,128)S(1)} %compare_convert_fusion, s32[32,2]{0,1:T(2,128)S(1)} %copy.12), kind=kOutput, calls=%fused_computation.5 | convolution fusion | flops 403178496 | bytes 17826304 | tf_op jit(solution)/shard_map/bjq,bjtf->qtf/dot_general | solution.py:33
  135.9 1.2 copy.13
  137.1 0.0 reduce-scatter.3.cloned.1.call-update
  137.1 0.0 all-gather.5.cloned.1.call-start
  137.1 37.1 %reduce-scatter.3.cloned.1.call-done = bf16[256,256]{1,0:T(8,128)(2,1)} async-done(((bf16[2048,256]{1,0:T(8,128)(2,1)}), bf16[256,256]{1,0:T(8,128)(2,1)}) %reduce-scatter.3.cloned.1.call-update) | async-done | bytes 131088 | tf_op jit(solution)/shard_map/reduce_scatter | solution.py:35
  174.3 0.0 copy-done
  174.3 0.0 copy-done.1
  174.3 1.8 multiply_convert_fusion
  176.1 0.9 convolution_convert_fusion
  177.0 0.0 all-gather.5.cloned.1.call-update
  177.0 0.0 all-reduce.2.cloned.1.call-start
  177.1 1.8 fusion.20
  178.9 0.0 all-reduce.2.cloned.1.call-update
  178.9 0.0 reduce-scatter.5.cloned.1.call-start
  179.0 39.0 %all-gather.5.cloned.1.call-done = bf16[2048,256]{1,0:T(8,128)(2,1)} async-done(((bf16[256,256]{1,0:T(8,128)(2,1)}), bf16[2048,256]{1,0:T(8,128)(2,1)}) %all-gather.5.cloned.1.call-update) | async-done | bytes 1048592 | tf_op jit(solution)/shard_map/all_gather | solution.py:48
  217.9 5.8 fusion.5
  223.7 30.2 %bitcast_convert_fusion = bf16[32,256,256]{1,2,0:T(8,128)(2,1)} fusion(bf16[32,2,256,256]{3,2,1,0:T(8,128)(2,1)} %bitcast.39, bf16[32,2,256,256]{3,0,2,1:T(8,128)(2,1)} %fusion.5), kind=kOutput, calls=%fused_computation.4 | convolution fusion | flops 2149580800 | bytes 20971520 | tf_op jit(solution)/shard_map/bjtu,bjtf->buf/dot_general | solution.py:59
  253.9 0.0 reduce-scatter.5.cloned.1.call-update
  253.9 221.2 %all-reduce.2.cloned.1.call-done = f32[256,256]{1,0:T(8,128)} async-done(((f32[256,256]{1,0:T(8,128)}), f32[256,256]{1,0:T(8,128)}) %all-reduce.2.cloned.1.call-update) | async-done | bytes 262160 | tf_op jit(solution)/shard_map/psum | solution.py:49
  475.2 131.2 %reduce-scatter.5.cloned.1.call-done = bf16[256,256]{1,0:T(8,128)(2,1)} async-done(((bf16[8192,256]{1,0:T(8,128)(2,1)}), bf16[256,256]{1,0:T(8,128)(2,1)}) %reduce-scatter.5.cloned.1.call-update) | async-done | bytes 131088 | tf_op jit(solution)/shard_map/reduce_scatter | solution.py:60
  606.4 1.7 copy.35
Async XLA Ops:
  7.2 167.1 %copy-start = (bf16[256,256]{1,0:T(8,128)(2,1)S(1)}, bf16[256,256]{1,0:T(8,128)(2,1)}, u32[]{:S(2)}) copy-start(bf16[256,256]{1,0:T(8,128)(2,1)} %param.10) | copy-start | bytes 393220
  7.2 93.4 %all-gather.3.cloned.1.call-start = ((), (), s32[]{:S(2)}) async-start(), calls=%async_computation.2 | async-start | bytes 4325376 | tf_op jit(solution)/shard_map/all_gather | solution.py:26
  7.9 166.3 %reduce-scatter.3.cloned.1.call-start = ((), (), s32[]{:S(2)}) async-start(), calls=%async_computation.3 | async-start | bytes 1179648 | tf_op jit(solution)/shard_map/reduce_scatter | solution.py:35
  113.3 61.0 %copy-start.1 = (bf16[256,256]{1,0:T(8,128)(2,1)S(1)}, bf16[256,256]{1,0:T(8,128)(2,1)}, u32[]{:S(2)}) copy-start(bf16[256,256]{1,0:T(8,128)(2,1)} %param.11) | copy-start | bytes 393220
  137.1 80.8 %all-gather.5.cloned.1.call-start = ((), (), s32[]{:S(2)}) async-start(), calls=%async_computation.4 | async-start | bytes 1179648 | tf_op jit(solution)/shard_map/all_gather | solution.py:48
  177.0 298.1 %all-reduce.2.cloned.1.call-start = ((), (), s32[]{:S(2)}) async-start(), calls=%async_computation.6 | async-start | bytes 524288 | tf_op jit(solution)/shard_map/psum | solution.py:49
  178.9 427.5 %reduce-scatter.5.cloned.1.call-start = ((), (), s32[]{:S(2)}) async-start(), calls=%async_computation.5 | async-start | bytes 4325376 | tf_op jit(solution)/shard_map/reduce_scatter | solution.py:60
Sparse Core Ops, SparseCore 0:
  10.8 89.7 all-gather.2
  137.2 37.0 reduce-scatter.2
  177.1 40.7 all-gather.4
  223.8 251.2 all-reduce.1
  479.8 126.5 reduce-scatter.4
where the time goes:
time: 615 us
  waiting for transfers between devices  519 us (84%)
  matrix products  75.8 us (12%)
  between operations  13.8 us (2%)
    psum x1, waiting for transfers between devices, local(): weight_grad = lax.psum(weight_term, ('row', 'rep'))  221 us
    reduce_scatter x1, waiting for transfers between devices, local(): lax.psum_scatter(result.reshape(count, width).astype(jnp.bfloat16), 'row'...  131 us
    all_gather x1, waiting for transfers between devices, local(): portion = lax.all_gather(features, 'row', axis=0, tiled=True)  90 us
    all_gather x1, waiting for transfers between devices, local(): dagg_full = lax.all_gather(dagg, 'rep', axis=0, tiled=True)  39 us
    reduce_scatter x1, waiting for transfers between devices, local(): lax.psum_scatter(partial_value.astype(jnp.bfloat16), 'rep', scatter_dimen...  37.1 us
    dot_general x1, matrix products, local(): jnp.einsum('bjtu,bjtf->buf', tile_part, picked, preferred_element_type=jn...  30.2 us
    dot_general x1, matrix products, local(): jnp.einsum('bjq,bjtf->qtf', select_part, products, precision=lax.Precisio...  22.6 us
    dot_general x1, matrix products, local(): jnp.einsum('bjtu,buf->bjtf', tile_part, source_rows, preferred_element_ty...  12.7 us
  transfers between devices with their start and end apart: 5, of which 5 were waited for; matrix products, arithmetic and copies ran while one was open for 7% of the time, Pallas kernels for 0%

commit v1 on v0

v1 whole, which is shorter than its diff:
```python
import jax
import jax.numpy as jnp
from jax import lax
from jax.experimental import pallas as pl
from jax.experimental.pallas import tpu as pltpu
from jax.sharding import PartitionSpec as P

MESH = pl.DeviceIdType.MESH
F32 = jnp.float32
BF16 = jnp.bfloat16
T = 256
HALF = 128
NZ = 8
NX = 4
NQ = 8
NC = 32
SLOTS = 64
TILE_PARTS = 8
SENDS = 128


def kernel(
    x_ref, tiles_ref, target_ref, count_ref, w_ref, ct_ref,
    hidden_ref, fgrad_ref, wgrad_ref,
    feat, tile, run, last_at, dt,
    b_half_out, b_half_in, b_full_out, b_full_in, b_y_out, b_y_in, b_keep,
    e_sib_out, e_sib_in, e_acc, e_far_out, e_half_in, e_out, e_in, e_y_out, e_y_in,
    w_term, w_in, w_a, w_b, w_c, w_sib_in, w_y_in, w_z_in, w_d, w_e, w_all,
    tile_sem, snd, rcv,
):
    row, rep = lax.axis_index("row"), lax.axis_index("rep")
    k, z, yh = row % 2, (row // 2) % NZ, row // (2 * NZ)
    x, yl = rep // 2, rep % 2

    def block(yh_, z_, k_):
        return yh_ * (2 * NZ) + z_ * 2 + k_

    me = row
    sib = (block(yh, z, 1 - k), rep)
    far_y = (block(1 - yh, z, k), rep)
    z_next = [(block(yh, (z + 1) % NZ, k), rep), (block(yh, (z + NZ - 1) % NZ, k), rep)]
    x_next = [(row, ((x + 1) % NX) * 2 + yl), (row, ((x + NX - 1) % NX) * 2 + yl)]
    near_y = (row, x * 2 + 1 - yl)

    def z_peer(d):
        return (block(yh, (z + d) % NZ, k), rep)

    def rep_peer(d):
        return (row, (rep + d) % NQ)

    number = {}
    started = []

    def sem_of(name):
        return number.setdefault(name, len(number))

    def post(name, src, dst, device):
        i = sem_of(name)
        copy = pltpu.make_async_remote_copy(
            src_ref=src, dst_ref=dst, send_sem=snd.at[i], recv_sem=rcv.at[i],
            device_id=device, device_id_type=MESH,
        )
        copy.start()
        started.append(copy)

    def arrive(name, dst, device):
        i = sem_of(name)
        pltpu.make_async_remote_copy(
            src_ref=dst, dst_ref=dst, send_sem=snd.at[i], recv_sem=rcv.at[i],
            device_id=device, device_id_type=MESH,
        ).wait_recv()

    loads = []
    per = SLOTS // TILE_PARTS
    for i in range(TILE_PARTS):
        copy = pltpu.make_async_copy(
            tiles_ref.at[pl.ds(i * per, per)], tile.at[pl.ds(i * per, per)], tile_sem.at[i]
        )
        copy.start()
        loads.append(copy)

    barrier = pltpu.get_barrier_semaphore()
    peers = [sib, far_y] + [z_peer(d) for d in range(1, NZ)] + [rep_peer(d) for d in range(1, NQ)]
    for peer in peers:
        pl.semaphore_signal(barrier, inc=1, device_id=peer, device_id_type=MESH)
    feat[me] = x_ref[...]
    run[SLOTS] = jnp.zeros((T, T), F32)
    dt[NQ] = jnp.zeros((T, T), BF16)
    pl.semaphore_wait(barrier, len(peers))

    rows_of = [pl.ds(0, HALF), pl.ds(HALF, HALF)]

    def yh_of(s):
        return yh if s == 0 else 1 - yh

    def z_at(way, t):
        return (z + NZ - t) % NZ if way == 0 else (z + t) % NZ

    def forward(c, p, last):
        prod = jnp.dot(
            tile[pl.ds(2 * c, 2)].reshape(2 * T, T), feat[c], preferred_element_type=F32
        )
        live = count_ref[0, c]
        for j in range(2):
            target = target_ref[0, 2 * c + j]
            before = jnp.int32(SLOTS)
            for q in range(NQ):
                before = jnp.where(target == q, last[q], before)
            run[2 * p + j] = prod[j * T : (j + 1) * T] + run[before]
            last = tuple(
                jnp.where((target == q) & (live > j), 2 * p + j, last[q]) for q in range(NQ)
            )
        return last

    def forward_group(last, start, size, t, core):
        def body(i, last):
            way, s = i % 2, i // 2
            if t == 0 or t == NZ // 2:
                way, s = 0, i
            zt = (z + jnp.where(way == 0, NZ - t, t)) % NZ
            c = block(jnp.where(s == 0, yh, 1 - yh), zt, core)
            return forward(c, start + i, last)

        return lax.fori_loop(0, size, body, last)

    post("ay", feat.at[me], feat.at[me], far_y)
    for way in range(2):
        post(("az", way, 1, 0), feat.at[me], feat.at[me], z_next[way])
    post(("as", 0, 0), feat.at[me], feat.at[me], sib)
    other = block(1 - yh, z, k)
    arrive("ay", feat.at[other], far_y)
    for way in range(2):
        post(("az", way, 1, 1), feat.at[other], feat.at[other], z_next[way])
    post(("as", 0, 1), feat.at[other], feat.at[other], sib)
    for copy in loads:
        copy.wait()
    last = (jnp.int32(SLOTS),) * NQ
    last = forward_group(last, 0, 2, 0, k)
    place = 2

    def sib_arrive(t):
        for s in range(2):
            if t == 0:
                c = block(yh_of(s), z, 1 - k)
                arrive(("as", 0, s), feat.at[c], sib)
                continue
            for way in range(2):
                c = block(yh_of(s), z_at(way, t), 1 - k)
                ref = feat.at[c, rows_of[way]] if t == NZ // 2 else feat.at[c]
                arrive(("as", t, s, way), ref, sib)

    for t in range(1, NZ // 2 + 1):
        for s in range(2):
            for way in range(2):
                c = block(yh_of(s), z_at(way, t), k)
                whole = feat.at[c]
                half = feat.at[c, rows_of[way]]
                ref = half if t == NZ // 2 else whole
                arrive(("az", way, t, s), ref, z_next[1 - way])
                if t < NZ // 2:
                    on = half if t + 1 == NZ // 2 else whole
                    post(("az", way, t + 1, s), on, on, z_next[way])
                post(("as", t, s, way), ref, ref, sib)
        size = 2 if t == NZ // 2 else 4
        last = forward_group(last, place, size, t, k)
        place += size
        sib_arrive(t - 1)
        size = 2 if t == 1 else 4
        last = forward_group(last, place, size, t - 1, 1 - k)
        place += size
    sib_arrive(NZ // 2)
    last = forward_group(last, place, 2, NZ // 2, 1 - k)
    for q in range(NQ):
        last_at[q] = last[q]

    def partial(q, rows):
        return run[last_at[q], rows]

    every = pl.ds(0, T)

    def yl_of(s):
        return 1 - yl if s == 0 else yl

    for s in range(2):
        for way in range(2):
            q = ((x + 2) % NX) * 2 + yl_of(s)
            i = 2 * s + way
            b_half_out[i] = partial(q, rows_of[way]).astype(BF16)
            post(("bh", i), b_half_out.at[i], b_half_in.at[i], x_next[way])
    for s in range(2):
        for way in range(2):
            q = ((x + (1 if way == 0 else NX - 1)) % NX) * 2 + yl
            if s == 0:
                q = q + 1 - 2 * yl
            i = 2 * s + way
            b_full_out[i, rows_of[1 - way]] = partial(q, rows_of[1 - way]).astype(BF16)
            arrive(("bh", i), b_half_in.at[i], x_next[1 - way])
            b_full_out[i, rows_of[way]] = (
                partial(q, rows_of[way]) + b_half_in[i].astype(F32)
            ).astype(BF16)
            post(("bf", i), b_full_out.at[i], b_full_in.at[i], x_next[way])
    for s in range(2):
        for way in range(2):
            arrive(("bf", 2 * s + way), b_full_in.at[2 * s + way], x_next[1 - way])
        total = (
            partial(x * 2 + yl_of(s), every)
            + b_full_in[2 * s].astype(F32)
            + b_full_in[2 * s + 1].astype(F32)
        )
        if s == 0:
            b_y_out[...] = total.astype(BF16)
            post("by", b_y_out, b_y_in, near_y)
        else:
            b_keep[...] = total
    arrive("by", b_y_in, near_y)
    agg = (b_keep[...] + b_y_in[...].astype(F32)).astype(BF16)

    pre = jnp.dot(agg, w_ref[...], preferred_element_type=F32)
    sigma = jax.nn.sigmoid(pre)
    grad_pre = (ct_ref[...].astype(F32) * sigma * (1.0 + pre * (1.0 - sigma))).astype(BF16)
    dt[rep] = lax.dot_general(
        w_ref[...], grad_pre, (((1,), (1,)), ((), ())), preferred_element_type=F32
    ).astype(BF16)

    own = dt.at[rep]
    post("dy", own, own, near_y)
    for way in range(2):
        post(("dx", way, 0), own, own, x_next[way])
    hidden_ref[...] = (pre * sigma).astype(BF16)
    near = dt.at[x * 2 + 1 - yl]
    arrive("dy", near, near_y)
    for way in range(2):
        post(("dx", way, 1), near, near, x_next[way])
    term = lax.dot_general(agg, grad_pre, (((0,), (0,)), ((), ())), preferred_element_type=F32)
    for q in range(NQ):
        for n in range(NZ):
            top, side = 32 * q + 8 * (n // 2), HALF * (n % 2)
            w_term[q, n] = term[top : top + 8, side : side + HALF]

    def dt_at(way, t, s):
        return ((x + (NX - t if way == 0 else t)) % NX) * 2 + (yl if s == 0 else 1 - yl)

    for s in range(2):
        for way in range(2):
            q = dt_at(way, 1, s)
            arrive(("dx", way, s), dt.at[q], x_next[1 - way])
            half = dt.at[q, rows_of[way]]
            post(("dh", way, s), half, half, x_next[way])
    for d in range(1, NQ):
        post(("w1", d), w_term.at[(rep + d) % NQ], w_in.at[d - 1], rep_peer(d))
    for s in range(2):
        for way in range(2):
            half = dt.at[dt_at(way, 2, s), rows_of[way]]
            arrive(("dh", way, s), half, x_next[1 - way])

    def backward(c):
        live = count_ref[0, c]
        picked = [
            dt[jnp.where(live > j, target_ref[0, 2 * c + j], NQ)] for j in range(2)
        ]
        return jnp.dot(
            jnp.concatenate(picked, axis=1), tile[pl.ds(2 * c, 2)].reshape(2 * T, T),
            preferred_element_type=F32,
        )

    base = {4: 0, 3: 2, 2: 6, 1: 10, 0: 14}
    count = {4: 2, 3: 4, 2: 4, 1: 4, 0: 2}

    def backward_group(t, core, store):
        def body(i, carry):
            way, s = i % 2, i // 2
            if t == 0 or t == NZ // 2:
                way, s = 0, i
            zt = (z + jnp.where(way == 0, t, NZ - t)) % NZ
            c = block(jnp.where(s == 0, 1 - yh, yh), zt, core)
            store(base[t] + i, backward(c))
            return carry

        lax.fori_loop(0, count[t], body, 0)

    def for_sib(t):
        def store(i, value):
            e_sib_out[i] = value.astype(BF16)

        backward_group(t, 1 - k, store)
        part = pl.ds(base[t], count[t])
        post(("es", t), e_sib_out.at[part], e_sib_in.at[part], sib)

    def for_own(t):
        def store(i, value):
            e_acc[i] = value

        backward_group(t, k, store)

    def sib_in(t):
        part = pl.ds(base[t], count[t])
        arrive(("es", t), e_sib_in.at[part], sib)

    def chip_sum(i, rows=every):
        return e_acc[i, rows] + e_sib_in[i, rows].astype(F32)

    def near_ring(t, s):
        for way in range(2):
            i = base[t] + 2 * s + way
            o = 4 * (3 - t) + 2 * s + way
            if t == 3:
                e_out[o, rows_of[1 - way]] = chip_sum(i, rows_of[1 - way]).astype(BF16)
                arrive(("eh", way, s), e_half_in.at[2 * s + way], z_next[1 - way])
                e_out[o, rows_of[way]] = (
                    chip_sum(i, rows_of[way]) + e_half_in[2 * s + way].astype(F32)
                ).astype(BF16)
            else:
                arrive(("er", o - 4), e_in.at[o - 4], z_next[1 - way])
                e_out[o] = (chip_sum(i) + e_in[o - 4].astype(F32)).astype(BF16)
            post(("er", o), e_out.at[o], e_in.at[o], z_next[way])

    for_sib(4)
    for_own(4)
    for_sib(3)
    sib_in(4)
    for s in range(2):
        e_far_out[s] = chip_sum(s).astype(BF16)
        for way in range(2):
            post(
                ("eh", way, s), e_far_out.at[s, rows_of[way]], e_half_in.at[2 * s + way],
                z_next[way],
            )
    for_own(3)
    for_sib(2)
    for d in range(1, NQ):
        arrive(("w1", d), w_in.at[d - 1], rep_peer(NQ - d))
    total = w_term[rep]
    for d in range(1, NQ):
        total = total + w_in[d - 1]
    w_a[...] = total
    post("w2", w_a, w_sib_in, sib)
    sib_in(3)
    near_ring(3, 0)
    arrive("w2", w_sib_in, sib)
    w_b[...] = w_a[...] + w_sib_in[...]
    post("w3", w_b, w_y_in, far_y)
    near_ring(3, 1)
    for_own(2)
    for_sib(1)
    arrive("w3", w_y_in, far_y)
    w_c[...] = w_b[...] + w_y_in[...]
    for d in range(1, NZ):
        post(("w4", d), w_c.at[(z + d) % NZ], w_z_in.at[d - 1], z_peer(d))
    sib_in(2)
    near_ring(2, 0)
    for d in range(1, NZ):
        arrive(("w4", d), w_z_in.at[d - 1], z_peer(NZ - d))
    total = w_c[z]
    for d in range(1, NZ):
        total = total + w_z_in[d - 1]
    w_e[z] = total
    for d in range(1, NZ):
        post(("w5", d), w_e.at[z], w_e.at[z], z_peer(d))
    near_ring(2, 1)
    for_own(1)
    for_sib(0)
    for_own(0)
    sib_in(1)
    near_ring(1, 0)
    for d in range(1, NZ):
        arrive(("w5", d), w_e.at[(z + NZ - d) % NZ], z_peer(NZ - d))
    for d in range(1, NQ):
        post(("w6", d), w_e, w_all.at[rep], rep_peer(d))
    w_all[rep] = w_e[...]
    near_ring(1, 1)
    sib_in(0)
    for s in range(2):
        for way in range(2):
            arrive(("er", 8 + 2 * s + way), e_in.at[8 + 2 * s + way], z_next[1 - way])
        total = (
            chip_sum(base[0] + s)
            + e_in[8 + 2 * s].astype(F32)
            + e_in[8 + 2 * s + 1].astype(F32)
        )
        if s == 0:
            e_y_out[...] = total.astype(BF16)
            post("ey", e_y_out, e_y_in, far_y)
        else:
            e_acc[0] = total
    for d in range(1, NQ):
        arrive(("w6", d), w_all.at[(rep + NQ - d) % NQ], rep_peer(NQ - d))
    for q in range(NQ):
        for n in range(NZ):
            top, side = 32 * q + 8 * (n // 2), HALF * (n % 2)
            wgrad_ref[top : top + 8, side : side + HALF] = w_all[q, n]
    arrive("ey", e_y_in, far_y)
    fgrad_ref[...] = (e_acc[0] + e_y_in[...].astype(F32)).T.astype(BF16)
    for copy in started:
        copy.wait_send()


def local(features, tiles, tile_target, tile_count, weight, cotangent):
    vmem = pl.BlockSpec(memory_space=pltpu.VMEM)
    smem = pl.BlockSpec(memory_space=pltpu.SMEM)
    anywhere = pl.BlockSpec(memory_space=pl.ANY)

    def buf(*shape, dtype=BF16):
        return pltpu.VMEM(shape, dtype)

    return pl.pallas_call(
        kernel,
        out_shape=(
            jax.ShapeDtypeStruct((T, T), BF16),
            jax.ShapeDtypeStruct((T, T), BF16),
            jax.ShapeDtypeStruct((T, T), F32),
        ),
        in_specs=[vmem, anywhere, smem, smem, vmem, vmem],
        out_specs=(vmem, vmem, vmem),
        scratch_shapes=[
            buf(NC, T, T),
            buf(SLOTS, T, T),
            buf(SLOTS + 1, T, T, dtype=F32),
            pltpu.SMEM((NQ,), jnp.int32),
            buf(NQ + 1, T, T),
            buf(4, HALF, T),
            buf(4, HALF, T),
            buf(4, T, T),
            buf(4, T, T),
            buf(T, T),
            buf(T, T),
            buf(T, T, dtype=F32),
            buf(16, T, T),
            buf(16, T, T),
            buf(16, T, T, dtype=F32),
            buf(2, T, T),
            buf(4, HALF, T),
            buf(12, T, T),
            buf(12, T, T),
            buf(T, T),
            buf(T, T),
            buf(NQ, NZ, 8, HALF, dtype=F32),
            buf(NQ - 1, NZ, 8, HALF, dtype=F32),
            buf(NZ, 8, HALF, dtype=F32),
            buf(NZ, 8, HALF, dtype=F32),
            buf(NZ, 8, HALF, dtype=F32),
            buf(NZ, 8, HALF, dtype=F32),
            buf(NZ, 8, HALF, dtype=F32),
            buf(NZ - 1, 8, HALF, dtype=F32),
            buf(8, HALF, dtype=F32),
            buf(NZ, 8, HALF, dtype=F32),
            buf(NQ, NZ, 8, HALF, dtype=F32),
            pltpu.SemaphoreType.DMA((TILE_PARTS,)),
            pltpu.SemaphoreType.DMA((SENDS,)),
            pltpu.SemaphoreType.DMA((SENDS,)),
        ],
        compiler_params=pltpu.CompilerParams(
            collective_id=0, has_side_effects=True, vmem_limit_bytes=56 * 1024 * 1024
        ),
        name="graph_layer",
    )(features, tiles, tile_target, tile_count, weight, cotangent)


def solution(mesh):
    return jax.shard_map(
        local,
        mesh=mesh,
        in_specs=(
            P(("row", "rep"), None),
            P(("row", "rep"), None, None),
            P(("row", "rep"), None),
            P(("row", "rep"), None),
            P(),
            P(("row", "rep"), None),
        ),
        out_specs=(P(("row", "rep"), None), P(("row", "rep"), None), P()),
        check_vma=False,
    )
```

time: 615 us -> 103 us (0.17)
  waiting for transfers between devices: 519 us -> 0 us
  Pallas kernels: 0 us -> 97.2 us
  matrix products: 75.8 us -> 0 us
  between operations: 13.8 us -> 0.64 us
    psum x1 -> x0, waiting for transfers between devices: 221 us -> none  [local(): weight_grad = lax.psum(weight_term, ('row', 'rep'))]
    reduce_scatter x2 -> x0, waiting for transfers between devices: 168 us -> none  [the longest x1 131 us: local(): lax.psum_scatter(result.reshape(count, width).astype(jnp.bfloat16), 'row'...]
    all_gather x2 -> x0, waiting for transfers between devices: 129 us -> none  [the longest x1 90 us: local(): portion = lax.all_gather(features, 'row', axis=0, tiled=True)]
    pallas_call x0 -> x1, Pallas kernels: none -> 97.2 us  [local(): pl.pallas_call(kernel, out_shape=(jax.ShapeDtypeStruct((T, T), BF16), jax...]
    dot_general x7 -> x0, matrix products: 75.8 us -> none  [the longest x1 30.2 us: local(): jnp.einsum('bjtu,bjtf->buf', tile_part, picked, preferred_element_type=jn...]
  transfers between devices with their start and end apart: 5 -> 0, of which waited for: 5 -> 0; matrix products, arithmetic and copies ran while one was open for 7% -> 0% of each run, Pallas kernels for 0% -> 0%
where the time goes in v1:
time: 103 us
  Pallas kernels  97.2 us (94%)
  local copies, waits for them, and re-layouts  4.8 us (5%)
    pallas_call x1, Pallas kernels, local(): pl.pallas_call(kernel, out_shape=(jax.ShapeDtypeStruct((T, T), BF16), jax...  97.2 us
    unnamed x3, local copies, waits for them, and re-layouts  4.8 us

profile of v1, /device:TPU:2, one launch (start us, length us, event | category | flops | bytes accessed | tf_op | source)
XLA Modules:
  0.0 102.6 jit_solution(11718790524721328542)
XLA Ops:
  0.6 97.2 %graph_layer.1 = (bf16[256,256]{1,0:T(8,128)(2,1)}, bf16[256,256]{1,0:T(8,128)(2,1)}, f32[256,256]{1,0:T(8,128)}) custom-call(bf16[256,256]{1,0:T(8,128)(2,1)} %x_ref.1, bf16[64,256,256]{2,1,0:T(8,128)(2,1)} %tiles_ref.1, s32[1,64]{1,0:T(1,128)} %target_ref.1, s32[1,32]{1,0:T(1,128)} %count_ref.1, bf16[256,256]{1,0:T(8,128)(2,1)} %w_ref.1, ...), custom_call_target="tpu_custom_call" | custom-call | tf_op jit(solution)/shard_map/graph_layer/pallas_call | solution.py:405
  97.8 1.6 %copy.12 = bf16[256,256]{1,0:T(8,128)(2,1)} copy(bf16[256,256]{1,0:T(8,128)(2,1)} %get-tuple-element.6) | data formatting | bytes 262144
  99.4 1.6 %copy.13 = bf16[256,256]{1,0:T(8,128)(2,1)} copy(bf16[256,256]{1,0:T(8,128)(2,1)} %get-tuple-element.7) | data formatting | bytes 262144
  101.0 1.7 %copy.14 = f32[256,256]{1,0:T(8,128)} copy(f32[256,256]{1,0:T(8,128)} %get-tuple-element.8) | data formatting | bytes 524288

commit v2 on v1

v2 whole, which is shorter than its diff:
```python
import jax
import jax.numpy as jnp
from jax import lax
from jax.experimental import pallas as pl
from jax.experimental.pallas import tpu as pltpu
from jax.sharding import PartitionSpec as P

MESH = pl.DeviceIdType.MESH
F32 = jnp.float32
BF16 = jnp.bfloat16
T = 256
HALF = 128
NZ = 8
NX = 4
NQ = 8
NC = 32
SLOTS = 64
TILE_PARTS = 8
SENDS = 192


def kernel(
    x_hbm, tiles_ref, target_hbm, count_hbm, w_hbm, ct_hbm,
    hidden_ref, fgrad_ref, wgrad_ref,
    target_ref, count_ref, w_ref, ct_ref, feat, tile, run, last_at, dt,
    ba_out, ba_in, bb_out, bb_in, bn_out, bn_in, by_out, by_in, b_keep,
    e_sib_out, e_sib_in, ea_out, ea_in, eb_out, eb_in, ef_out, ef_in, ey_out, ey_in,
    w_term, w_in, w_a, w_b, w_c, w_z_in, w_e, w_all,
    tile_sem, in_sem, snd, rcv,
):
    row, rep = lax.axis_index("row"), lax.axis_index("rep")
    k, z, yh = row % 2, (row // 2) % NZ, row // (2 * NZ)
    x, yl = rep // 2, rep % 2

    def block(yh_, z_, k_):
        return yh_ * (2 * NZ) + z_ * 2 + k_

    me = row
    sib = (block(yh, z, 1 - k), rep)
    far_y = (block(1 - yh, z, k), rep)
    group = [sib, far_y, (block(1 - yh, z, 1 - k), rep)]
    z_next = [(block(yh, (z + 1) % NZ, k), rep), (block(yh, (z + NZ - 1) % NZ, k), rep)]
    x_next = [(row, ((x + 1) % NX) * 2 + yl), (row, ((x + NX - 1) % NX) * 2 + yl)]
    near_y = (row, x * 2 + 1 - yl)

    def z_peer(d):
        return (block(yh, (z + d) % NZ, k), rep)

    def rep_peer(d):
        return (row, (rep + d) % NQ)

    number = {}
    started = []

    def sem_of(name):
        return number.setdefault(name, len(number))

    def post(name, src, dst, device):
        i = sem_of(name)
        copy = pltpu.make_async_remote_copy(
            src_ref=src, dst_ref=dst, send_sem=snd.at[i], recv_sem=rcv.at[i],
            device_id=device, device_id_type=MESH,
        )
        copy.start()
        started.append(copy)

    def arrive(name, dst, device):
        i = sem_of(name)
        pltpu.make_async_remote_copy(
            src_ref=dst, dst_ref=dst, send_sem=snd.at[i], recv_sem=rcv.at[i],
            device_id=device, device_id_type=MESH,
        ).wait_recv()

    inputs = [
        (x_hbm.at[:, pl.ds(0, HALF)], feat.at[0, me]),
        (x_hbm.at[:, pl.ds(HALF, HALF)], feat.at[1, me]),
        (target_hbm, target_ref),
        (count_hbm, count_ref),
        (w_hbm, w_ref),
        (ct_hbm, ct_ref),
    ]
    inputs = [
        pltpu.make_async_copy(src, dst, in_sem.at[i]) for i, (src, dst) in enumerate(inputs)
    ]
    for copy in inputs:
        copy.start()
    loads = []
    per = SLOTS // TILE_PARTS
    for i in range(TILE_PARTS):
        copy = pltpu.make_async_copy(
            tiles_ref.at[pl.ds(i * per, per)], tile.at[pl.ds(i * per, per)], tile_sem.at[i]
        )
        copy.start()
        loads.append(copy)

    barrier = pltpu.get_barrier_semaphore()
    peers = group + [z_peer(d) for d in range(1, NZ)] + [rep_peer(d) for d in range(1, NQ)]
    for peer in peers:
        pl.semaphore_signal(barrier, inc=1, device_id=peer, device_id_type=MESH)
    run[SLOTS] = jnp.zeros((T, T), F32)
    dt[NQ] = jnp.zeros((T, T), BF16)
    pl.semaphore_wait(barrier, len(peers))

    rows_of = [pl.ds(0, HALF), pl.ds(HALF, HALF)]
    FAR = NZ // 2

    def yh_of(s):
        return yh if s == 0 else 1 - yh

    def z_at(way, t):
        return (z + NZ - t) % NZ if way == 0 else (z + t) % NZ

    def tags(h, t, s):
        if t == 0:
            return [0]
        if t == FAR and h == 0:
            return [s]
        return [0, 1]

    def piece(h, t, s, tag, core, split):
        c = block(yh_of(s), z_at(tag, t), core)
        if split:
            return feat.at[h, c, rows_of[tag]]
        return feat.at[h, c]

    def forward(c, p, last):
        prod = jnp.dot(
            tile[pl.ds(2 * c, 2)].reshape(2 * T, T),
            jnp.concatenate([feat[0, c], feat[1, c]], axis=1),
            preferred_element_type=F32,
        )
        live = count_ref[0, c]
        for j in range(2):
            target = target_ref[0, 2 * c + j]
            before = jnp.int32(SLOTS)
            for q in range(NQ):
                before = jnp.where(target == q, last[q], before)
            run[2 * p + j] = prod[j * T : (j + 1) * T] + run[before]
            last = tuple(
                jnp.where((target == q) & (live > j), 2 * p + j, last[q]) for q in range(NQ)
            )
        return last

    state = {"last": (jnp.int32(SLOTS),) * NQ, "place": 0}

    def compute(t, s, core):
        start = state["place"]
        size = 1 if t in (0, FAR) else 2

        def body(i, last):
            zt = (z + jnp.where(i == 0, NZ - t, t)) % NZ
            return forward(block(yh_of(s), zt, core), start + i, last)

        state["last"] = lax.fori_loop(0, size, body, state["last"])
        state["place"] = start + size

    def split_at(h, t):
        return h == 1 and t == FAR

    def z_post(h, s, t, tag):
        ref = piece(h, t - 1, s, tag, k, split_at(h, t))
        post(("az", h, s, t, tag), ref, ref, z_next[tag])

    def sib_post(h, t, s, tag):
        ref = piece(h, t, s, tag, k, split_at(h, t))
        post(("as", h, t, s, tag), ref, ref, sib)

    def far_post(t, tag):
        ref = piece(1, t, 0, tag, k, split_at(1, t))
        post(("af", t, tag), ref, ref, far_y)

    def sib_wait(t, s):
        for h in range(2):
            for tag in tags(h, t, s):
                arrive(
                    ("as", h, t, s, tag), piece(h, t, s, tag, 1 - k, split_at(h, t)), sib
                )

    for copy in inputs[:2]:
        copy.wait()
    own = feat.at[0, me]
    post("ay", own, own, far_y)
    for h in range(2):
        for way in range(2):
            z_post(h, 0, 1, way)
    far_post(0, 0)
    for h in range(2):
        sib_post(h, 0, 0, 0)
    arrive("ay", piece(0, 0, 1, 0, k, False), far_y)
    for way in range(2):
        z_post(0, 1, 1, way)
    sib_post(0, 0, 1, 0)
    for copy in inputs[2:4] + loads:
        copy.wait()
    compute(0, 0, k)
    def z_step(h, s, t):
        for tag in tags(h, t, s):
            ref = piece(h, t, s, tag, k, split_at(h, t))
            arrive(("az", h, s, t, tag), ref, z_next[1 - tag])
            if t < FAR and tag in tags(h, t + 1, s):
                z_post(h, s, t + 1, tag)
            if h == 1:
                far_post(t, tag)
            sib_post(h, t, s, tag)

    for t in range(1, FAR + 3):
        if t <= FAR:
            z_step(1, 0, t)
            z_step(0, 0, t)
        if t >= 2:
            sib_wait(t - 2, 1)
            compute(t - 2, 1, 1 - k)
        if t - 1 <= FAR:
            sib_wait(t - 1, 0)
            compute(t - 1, 0, 1 - k)
        if t <= FAR:
            z_step(0, 1, t)
        if t - 1 <= FAR:
            for tag in tags(1, t - 1, 1):
                arrive(("af", t - 1, tag), piece(1, t - 1, 1, tag, k, split_at(1, t - 1)), far_y)
                sib_post(1, t - 1, 1, tag)
        if t <= FAR:
            compute(t, 0, k)
        if t - 1 <= FAR:
            compute(t - 1, 1, k)
    for q in range(NQ):
        last_at[q] = state["last"][q]

    every = pl.ds(0, T)

    def partial(q, h):
        return run[last_at[q], :, h * HALF : (h + 1) * HALF]

    def q_at(way, t, s):
        return ((x + (t if way == 0 else NX - t)) % NX) * 2 + (1 - yl if s == 0 else yl)

    def near_post(i, q):
        bn_out[i] = partial(q, 1).astype(BF16)
        post(("bn", i), bn_out.at[i], bn_in.at[i], near_y)

    def a_post(i, value, way):
        ba_out[i] = value.astype(BF16)
        post(("ba", i), ba_out.at[i], ba_in.at[i], x_next[way])

    near_post(0, q_at(0, 2, 0))
    for s in range(2):
        a_post(s, partial(q_at(0, 2, s), 0), s)
    for way in range(2):
        near_post(1 + way, q_at(way, 1, 0))
    for s in range(2):
        way = 1 - s
        a_post(2 + 2 * s + way, partial(q_at(way, 1, s), 0), way)
    near_post(3, q_at(0, 0, 0))
    for s in range(2):
        arrive(("ba", s), ba_in.at[s], x_next[1 - s])
        a_post(2 + 3 * s, partial(q_at(s, 1, s), 0) + ba_in[s].astype(F32), s)
    arrive(("bn", 0), bn_in.at[0], near_y)
    bb_out[0] = (partial(q_at(0, 2, 1), 1) + bn_in[0].astype(F32)).astype(BF16)
    for way in range(2):
        post(
            ("bh", way), bb_out.at[0, rows_of[way]], bb_in.at[0, rows_of[way]], x_next[way]
        )
    for way in range(2):
        arrive(("bn", 1 + way), bn_in.at[1 + way], near_y)
        arrive(("bh", way), bb_in.at[0, rows_of[way]], x_next[1 - way])
        value = partial(q_at(way, 1, 1), 1) + bn_in[1 + way].astype(F32)
        extra = bb_in[0, rows_of[way]].astype(F32)
        keep, more = slice((1 - way) * HALF, (2 - way) * HALF), slice(way * HALF, (1 + way) * HALF)
        bb_out[1 + way, rows_of[1 - way]] = value[keep].astype(BF16)
        bb_out[1 + way, rows_of[way]] = (value[more] + extra).astype(BF16)
        post(("bb", way), bb_out.at[1 + way], bb_in.at[1 + way], x_next[way])
    for s in range(2):
        for way in range(2):
            i = 2 + 2 * s + way
            arrive(("ba", i), ba_in.at[i], x_next[1 - way])
        total = (
            partial(q_at(0, 0, s), 0)
            + ba_in[2 + 2 * s].astype(F32) + ba_in[3 + 2 * s].astype(F32)
        )
        if s == 0:
            by_out[...] = total.astype(BF16)
            post("by", by_out, by_in, near_y)
        else:
            b_keep[:, :HALF] = total
    arrive(("bn", 3), bn_in.at[3], near_y)
    for way in range(2):
        arrive(("bb", way), bb_in.at[1 + way], x_next[1 - way])
    b_keep[:, HALF:] = (
        partial(q_at(0, 0, 1), 1) + bn_in[3].astype(F32)
        + bb_in[1].astype(F32) + bb_in[2].astype(F32)
    )
    arrive("by", by_in, near_y)
    b_keep[:, :HALF] = b_keep[:, :HALF] + by_in[...].astype(F32)
    agg = b_keep[...].astype(BF16)

    for copy in inputs[4:]:
        copy.wait()
    pre = jnp.dot(agg, w_ref[...], preferred_element_type=F32)
    sigma = jax.nn.sigmoid(pre)
    grad_pre = (ct_ref[...].astype(F32) * sigma * (1.0 + pre * (1.0 - sigma))).astype(BF16)
    dt[rep] = lax.dot_general(
        w_ref[...], grad_pre, (((1,), (1,)), ((), ())), preferred_element_type=F32
    ).astype(BF16)

    sub_of = [pl.ds(HALF, HALF // 2), pl.ds(HALF + HALF // 2, HALF // 2)]

    def dt_at(way, t, s):
        return ((x + (NX - t if way == 0 else t)) % NX) * 2 + (yl if s == 0 else 1 - yl)

    def hop(name, ref, device):
        post(name, ref, ref, device)

    top, low = dt.at[rep, rows_of[0]], dt.at[rep, rows_of[1]]
    hop("dy", top, near_y)
    for way in range(2):
        hop(("da", 1, 0, way), top, x_next[way])
        hop(("db", 1, way), low, x_next[way])
    hop(("dn", 0), low, near_y)
    hidden_ref[...] = (pre * sigma).astype(BF16)
    near = dt.at[dt_at(0, 0, 1), rows_of[0]]
    arrive("dy", near, near_y)
    for way in range(2):
        hop(("da", 1, 1, way), near, x_next[way])
    term = lax.dot_general(agg, grad_pre, (((0,), (0,)), ((), ())), preferred_element_type=F32)
    for q in range(NQ):
        for n in range(NZ):
            up, side = 32 * q + 8 * (n // 2), HALF * (n % 2)
            w_term[q, n] = term[up : up + 8, side : side + HALF]

    for way in range(2):
        ref = dt.at[dt_at(way, 1, 0), rows_of[0]]
        arrive(("da", 1, 0, way), ref, x_next[1 - way])
        if way == 0:
            hop(("da", 2, 0), ref, x_next[way])
        q = dt_at(way, 1, 0)
        arrive(("db", 1, way), dt.at[q, rows_of[1]], x_next[1 - way])
        hop(("db", 2, way), dt.at[q, sub_of[way]], x_next[way])
        hop(("dn", 1 + way), dt.at[q, rows_of[1]], near_y)
    for way in (1, 0):
        ref = dt.at[dt_at(way, 1, 1), rows_of[0]]
        arrive(("da", 1, 1, way), ref, x_next[1 - way])
        if way == 1:
            hop(("da", 2, 1), ref, x_next[way])
    for way in range(2):
        ref = dt.at[dt_at(way, 2, 0), sub_of[way]]
        arrive(("db", 2, way), ref, x_next[1 - way])
        hop(("dn", 3 + way), ref, near_y)
    for d in range(1, NQ):
        post(("w1", d), w_term.at[(rep + d) % NQ], w_in.at[d - 1], rep_peer(d))
    for s in range(2):
        arrive(("da", 2, s), dt.at[dt_at(s, 2, s), rows_of[0]], x_next[1 - s])
    arrive(("dn", 0), dt.at[dt_at(0, 0, 1), rows_of[1]], near_y)
    for way in range(2):
        arrive(("dn", 1 + way), dt.at[dt_at(way, 1, 1), rows_of[1]], near_y)
    for way in range(2):
        arrive(("dn", 3 + way), dt.at[dt_at(way, 2, 1), sub_of[way]], near_y)

    def backward(c):
        live = count_ref[0, c]
        picked = [
            dt[jnp.where(live > j, target_ref[0, 2 * c + j], NQ)] for j in range(2)
        ]
        return jnp.dot(
            jnp.concatenate(picked, axis=1), tile[pl.ds(2 * c, 2)].reshape(2 * T, T),
            preferred_element_type=F32,
        )

    base = {4: 0, 3: 2, 2: 6, 1: 10, 0: 14}
    count = {4: 2, 3: 4, 2: 4, 1: 4, 0: 2}

    def backward_group(t, core, store):
        def body(i, carry):
            way, s = i % 2, i // 2
            if t == 0 or t == NZ // 2:
                way, s = 0, i
            zt = (z + jnp.where(way == 0, t, NZ - t)) % NZ
            c = block(jnp.where(s == 0, 1 - yh, yh), zt, core)
            store(base[t] + i, backward(c))
            return carry

        lax.fori_loop(0, count[t], body, 0)

    def for_sib(t):
        def store(i, value):
            e_sib_out[i] = value.astype(BF16)

        backward_group(t, 1 - k, store)
        part = pl.ds(base[t], count[t])
        post(("es", t), e_sib_out.at[part], e_sib_in.at[part], sib)

    def for_own(t):
        def store(i, value):
            run[i] = value

        backward_group(t, k, store)

    def sib_in(t):
        part = pl.ds(base[t], count[t])
        arrive(("es", t), e_sib_in.at[part], sib)

    def chip_sum(i, h):
        rows = rows_of[h]
        return run[i, rows] + e_sib_in[i, rows].astype(F32)

    quarter = HALF // 2

    def far_sum_post(t):
        for way in range(1 if t in (0, FAR) else 2):
            o = 0 if t == FAR else 7 if t == 0 else 1 + 2 * (3 - t) + way
            ef_out[o] = chip_sum(base[t] + way, 1).astype(BF16)
            post(("ef", o), ef_out.at[o], ef_in.at[o], far_y)

    def low_sum(t, way):
        o = 0 if t == FAR else 7 if t == 0 else 1 + 2 * (3 - t) + way
        arrive(("ef", o), ef_in.at[o], far_y)
        i = base[t] + (1 if t in (0, FAR) else 2 + way)
        return chip_sum(i, 1) + ef_in[o].astype(F32)

    def ring_top(t, s):
        if t == FAR:
            ea_out[s] = chip_sum(base[t] + s, 0).astype(BF16)
            post(("ea", s), ea_out.at[s], ea_in.at[s], z_next[s])
            return
        for way in (1 - s, s):
            value = chip_sum(base[t] + 2 * s + way, 0)
            o = 2 + 4 * (3 - t) + 2 * s + way
            before = o - 4 if t < 3 else s if way == s else None
            if before is not None:
                arrive(("ea", before), ea_in.at[before], z_next[1 - way])
                value = value + ea_in[before].astype(F32)
            ea_out[o] = value.astype(BF16)
            post(("ea", o), ea_out.at[o], ea_in.at[o], z_next[way])

    def ring_low(t):
        if t == FAR:
            eb_out[0] = low_sum(t, 0).astype(BF16)
            for way in range(2):
                part = pl.ds(way * quarter, quarter)
                post(("eh", way), eb_out.at[0, part], eb_in.at[0, part], z_next[way])
            return
        for way in range(2):
            value = low_sum(t, way)
            o = 1 + 2 * (3 - t) + way
            if t == 3:
                part = pl.ds(way * quarter, quarter)
                arrive(("eh", way), eb_in.at[0, part], z_next[1 - way])
                more = value[way * quarter : (way + 1) * quarter] + eb_in[0, part].astype(F32)
                keep = value[(1 - way) * quarter : (2 - way) * quarter]
                eb_out[o, part] = more.astype(BF16)
                eb_out[o, pl.ds((1 - way) * quarter, quarter)] = keep.astype(BF16)
            else:
                arrive(("eb", o - 2), eb_in.at[o - 2], z_next[1 - way])
                eb_out[o] = (value + eb_in[o - 2].astype(F32)).astype(BF16)
            post(("eb", o), eb_out.at[o], eb_in.at[o], z_next[way])

    for_sib(4)
    for_own(4)
    for_sib(3)
    sib_in(4)
    far_sum_post(4)
    ring_top(4, 0)
    ring_top(4, 1)
    for_own(3)
    sib_in(3)
    far_sum_post(3)
    ring_top(3, 0)
    ring_top(3, 1)
    for_sib(2)
    for d in range(1, NQ):
        arrive(("w1", d), w_in.at[d - 1], rep_peer(NQ - d))
    total = w_term[rep]
    for d in range(1, NQ):
        total = total + w_in[d - 1]
    w_a[...] = total
    for i in range(3):
        post(("w2", i), w_a, w_b.at[i], group[i])
    ring_low(4)
    for_own(2)
    sib_in(2)
    far_sum_post(2)
    ring_top(2, 0)
    ring_top(2, 1)
    for_sib(1)
    for i in range(3):
        arrive(("w2", i), w_b.at[i], group[i])
    w_c[...] = (w_a[...] + w_b[0]) + (w_b[1] + w_b[2])
    for d in range(1, NZ):
        post(("w4", d), w_c.at[(z + d) % NZ], w_z_in.at[d - 1], z_peer(d))
    ring_low(3)
    for_own(1)
    sib_in(1)
    far_sum_post(1)
    ring_top(1, 0)
    for_sib(0)
    for d in range(1, NZ):
        arrive(("w4", d), w_z_in.at[d - 1], z_peer(NZ - d))
    total = w_c[z]
    for d in range(1, NZ):
        total = total + w_z_in[d - 1]
    w_e[z] = total
    for d in range(1, NZ):
        post(("w5", d), w_e.at[z], w_e.at[z], z_peer(d))
    ring_top(1, 1)
    for_own(0)
    sib_in(0)
    far_sum_post(0)
    ring_low(2)
    for d in range(1, NZ):
        arrive(("w5", d), w_e.at[(z + NZ - d) % NZ], z_peer(NZ - d))
    for d in range(1, NQ):
        post(("w6", d), w_e, w_all.at[rep], rep_peer(d))
    w_all[rep] = w_e[...]
    ring_low(1)
    for s in range(2):
        i = 10 + 2 * s
        for way in range(2):
            arrive(("ea", i + way), ea_in.at[i + way], z_next[1 - way])
        total = (
            chip_sum(base[0] + s, 0) + ea_in[i].astype(F32) + ea_in[i + 1].astype(F32)
        )
        if s == 0:
            ey_out[...] = total.astype(BF16)
            post("ey", ey_out, ey_in, far_y)
        else:
            run[0, rows_of[0]] = total
    low_total = low_sum(0, 0)
    for way in range(2):
        arrive(("eb", 5 + way), eb_in.at[5 + way], z_next[1 - way])
    low_total = low_total + eb_in[5].astype(F32) + eb_in[6].astype(F32)
    fgrad_ref[:, HALF:] = low_total.T.astype(BF16)
    for d in range(1, NQ):
        arrive(("w6", d), w_all.at[(rep + NQ - d) % NQ], rep_peer(NQ - d))
    for q in range(NQ):
        for n in range(NZ):
            up, side = 32 * q + 8 * (n // 2), HALF * (n % 2)
            wgrad_ref[up : up + 8, side : side + HALF] = w_all[q, n]
    arrive("ey", ey_in, far_y)
    fgrad_ref[:, :HALF] = (run[0, rows_of[0]] + ey_in[...].astype(F32)).T.astype(BF16)
    for copy in started:
        copy.wait_send()


def local(features, tiles, tile_target, tile_count, weight, cotangent):
    vmem = pl.BlockSpec(memory_space=pltpu.VMEM)
    hbm = pl.BlockSpec(memory_space=pltpu.HBM)

    def buf(*shape, dtype=BF16):
        return pltpu.VMEM(shape, dtype)

    return pl.pallas_call(
        kernel,
        out_shape=(
            jax.ShapeDtypeStruct((T, T), BF16),
            jax.ShapeDtypeStruct((T, T), BF16),
            jax.ShapeDtypeStruct((T, T), F32),
        ),
        in_specs=[hbm] * 6,
        out_specs=(vmem, vmem, vmem),
        scratch_shapes=[
            pltpu.SMEM((1, SLOTS), jnp.int32),
            pltpu.SMEM((1, NC), jnp.int32),
            buf(T, T),
            buf(T, T),
            buf(2, NC, T, HALF),
            buf(SLOTS, T, T),
            buf(SLOTS + 1, T, T, dtype=F32),
            pltpu.SMEM((NQ,), jnp.int32),
            buf(NQ + 1, T, T),
            buf(6, T, HALF),
            buf(6, T, HALF),
            buf(3, T, HALF),
            buf(3, T, HALF),
            buf(4, T, HALF),
            buf(4, T, HALF),
            buf(T, HALF),
            buf(T, HALF),
            buf(T, T, dtype=F32),
            buf(16, T, T),
            buf(16, T, T),
            buf(14, HALF, T),
            buf(14, HALF, T),
            buf(7, HALF, T),
            buf(7, HALF, T),
            buf(8, HALF, T),
            buf(8, HALF, T),
            buf(HALF, T),
            buf(HALF, T),
            buf(NQ, NZ, 8, HALF, dtype=F32),
            buf(NQ - 1, NZ, 8, HALF, dtype=F32),
            buf(NZ, 8, HALF, dtype=F32),
            buf(3, NZ, 8, HALF, dtype=F32),
            buf(NZ, 8, HALF, dtype=F32),
            buf(NZ - 1, 8, HALF, dtype=F32),
            buf(NZ, 8, HALF, dtype=F32),
            buf(NQ, NZ, 8, HALF, dtype=F32),
            pltpu.SemaphoreType.DMA((TILE_PARTS,)),
            pltpu.SemaphoreType.DMA((6,)),
            pltpu.SemaphoreType.DMA((SENDS,)),
            pltpu.SemaphoreType.DMA((SENDS,)),
        ],
        compiler_params=pltpu.CompilerParams(
            collective_id=0, has_side_effects=True, vmem_limit_bytes=46 * 1024 * 1024
        ),
        name="graph_layer",
    )(*[
        pltpu.with_memory_space_constraint(value, pltpu.HBM)
        for value in (features, tiles, tile_target, tile_count, weight, cotangent)
    ])


def solution(mesh):
    return jax.shard_map(
        local,
        mesh=mesh,
        in_specs=(
            P(("row", "rep"), None),
            P(("row", "rep"), None, None),
            P(("row", "rep"), None),
            P(("row", "rep"), None),
            P(),
            P(("row", "rep"), None),
        ),
        out_specs=(P(("row", "rep"), None), P(("row", "rep"), None), P()),
        check_vma=False,
    )
```

time: 103 us -> 93.1 us (0.904); the launches traced: 103 us -> 91.6 us
  Pallas kernels: 97.2 us -> 89 us
  local copies, waits for them, and re-layouts: 4.8 us -> 2.01 us
    pallas_call x1, Pallas kernels: 97.2 us -> 89 us  [local(): pl.pallas_call(kernel, out_shape=(jax.ShapeDtypeStruct((T, T), BF16), jax...]
    unnamed x3, local copies, waits for them, and re-layouts: 4.8 us -> 2.01 us
where the time goes in v2:
time: 93.1 us; the launch traced here: 91.6 us
  Pallas kernels  89 us (96%)
  local copies, waits for them, and re-layouts  2.01 us (2%)
    pallas_call x1, Pallas kernels, local(): pl.pallas_call(kernel, out_shape=(jax.ShapeDtypeStruct((T, T), BF16), jax...  89 us
    unnamed x3, local copies, waits for them, and re-layouts  2.01 us

profile of v2, /device:TPU:2, one launch (start us, length us, event | category | flops | bytes accessed | tf_op | source)
XLA Modules:
  0.0 91.6 jit_solution(7844219068390090463)
XLA Ops:
  0.6 89.0 %graph_layer.1 = (bf16[256,256]{1,0:T(8,128)(2,1)S(1)}, bf16[256,256]{1,0:T(8,128)(2,1)S(1)}, f32[256,256]{1,0:T(8,128)S(1)}) custom-call(bf16[256,256]{1,0:T(8,128)(2,1)} %x_hbm.1, bf16[64,256,256]{2,1,0:T(8,128)(2,1)} %tiles_ref.1, s32[1,64]{1,0:T(1,128)} %target_hbm.1, s32[1,32]{1,0:T(1,128)} %count_hbm.1, bf16[256,256]{1,0:T(8,128)(2,1)} %w_hbm.1, ...), custom_call_target="tpu_custom_call" | custom-call | tf_op jit(solution)/shard_map/graph_layer/pallas_call | solution.py:550
  89.6 0.7 copy.12
  90.3 0.7 copy.13
  90.9 0.7 copy.14

commit v3 on v2

--- a/solution.py
+++ b/solution.py
@@ -323,9 +323,11 @@
         hop(("da", 1, 1, way), near, x_next[way])
     term = lax.dot_general(agg, grad_pre, (((0,), (0,)), ((), ())), preferred_element_type=F32)
     for q in range(NQ):
+        pieces = []
         for n in range(NZ):
             up, side = 32 * q + 8 * (n // 2), HALF * (n % 2)
-            w_term[q, n] = term[up : up + 8, side : side + HALF]
+            pieces.append(term[up : up + 8, side : side + HALF])
+        w_term[q] = jnp.concatenate(pieces, axis=0).astype(BF16)
 
     for way in range(2):
         ref = dt.at[dt_at(way, 1, 0), rows_of[0]]
@@ -453,6 +455,40 @@
                 eb_out[o] = (value + eb_in[o - 2].astype(F32)).astype(BF16)
             post(("eb", o), eb_out.at[o], eb_in.at[o], z_next[way])
 
+    def sum_rep():
+        for d in range(1, NQ):
+            arrive(("w1", d), w_in.at[d - 1], rep_peer(NQ - d))
+        total = w_term[rep].astype(F32)
+        for d in range(1, NQ):
+            total = total + w_in[d - 1].astype(F32)
+        w_a[...] = total.reshape(NZ, 8, HALF)
+        for i in range(3):
+            post(("w2", i), w_a, w_b.at[i], group[i])
+
+    def sum_group():
+        for i in range(3):
+            arrive(("w2", i), w_b.at[i], group[i])
+        w_c[...] = (w_a[...] + w_b[0]) + (w_b[1] + w_b[2])
+        for d in range(1, NZ):
+            post(("w4", d), w_c.at[(z + d) % NZ], w_z_in.at[d - 1], z_peer(d))
+
+    def sum_z():
+        for d in range(1, NZ):
+            arrive(("w4", d), w_z_in.at[d - 1], z_peer(NZ - d))
+        total = w_c[z]
+        for d in range(1, NZ):
+            total = total + w_z_in[d - 1]
+        w_e[z] = total
+        for d in range(1, NZ):
+            post(("w5", d), w_e.at[z], w_e.at[z], z_peer(d))
+
+    def spread_rep():
+        for d in range(1, NZ):
+            arrive(("w5", d), w_e.at[(z + NZ - d) % NZ], z_peer(NZ - d))
+        w_all[rep] = w_e[...].reshape(NZ * 8, HALF).astype(BF16)
+        for d in range(1, NQ):
+            post(("w6", d), w_all.at[rep], w_all.at[rep], rep_peer(d))
+
     for_sib(4)
     for_own(4)
     for_sib(3)
@@ -463,53 +499,31 @@
     for_own(3)
     sib_in(3)
     far_sum_post(3)
+    for_sib(2)
     ring_top(3, 0)
     ring_top(3, 1)
-    for_sib(2)
-    for d in range(1, NQ):
-        arrive(("w1", d), w_in.at[d - 1], rep_peer(NQ - d))
-    total = w_term[rep]
-    for d in range(1, NQ):
-        total = total + w_in[d - 1]
-    w_a[...] = total
-    for i in range(3):
-        post(("w2", i), w_a, w_b.at[i], group[i])
+    sum_rep()
     ring_low(4)
     for_own(2)
     sib_in(2)
     far_sum_post(2)
+    for_sib(1)
     ring_top(2, 0)
     ring_top(2, 1)
-    for_sib(1)
-    for i in range(3):
-        arrive(("w2", i), w_b.at[i], group[i])
-    w_c[...] = (w_a[...] + w_b[0]) + (w_b[1] + w_b[2])
-    for d in range(1, NZ):
-        post(("w4", d), w_c.at[(z + d) % NZ], w_z_in.at[d - 1], z_peer(d))
+    sum_group()
     ring_low(3)
     for_own(1)
     sib_in(1)
     far_sum_post(1)
+    for_sib(0)
+    for_own(0)
     ring_top(1, 0)
-    for_sib(0)
-    for d in range(1, NZ):
-        arrive(("w4", d), w_z_in.at[d - 1], z_peer(NZ - d))
-    total = w_c[z]
-    for d in range(1, NZ):
-        total = total + w_z_in[d - 1]
-    w_e[z] = total
-    for d in range(1, NZ):
-        post(("w5", d), w_e.at[z], w_e.at[z], z_peer(d))
+    sum_z()
     ring_top(1, 1)
-    for_own(0)
     sib_in(0)
     far_sum_post(0)
     ring_low(2)
-    for d in range(1, NZ):
-        arrive(("w5", d), w_e.at[(z + NZ - d) % NZ], z_peer(NZ - d))
-    for d in range(1, NQ):
-        post(("w6", d), w_e, w_all.at[rep], rep_peer(d))
-    w_all[rep] = w_e[...]
+    spread_rep()
     ring_low(1)
     for s in range(2):
         i = 10 + 2 * s
@@ -531,9 +545,10 @@
     for d in range(1, NQ):
         arrive(("w6", d), w_all.at[(rep + NQ - d) % NQ], rep_peer(NQ - d))
     for q in range(NQ):
+        done = w_all[q].astype(F32)
         for n in range(NZ):
             up, side = 32 * q + 8 * (n // 2), HALF * (n % 2)
-            wgrad_ref[up : up + 8, side : side + HALF] = w_all[q, n]
+            wgrad_ref[up : up + 8, side : side + HALF] = done[8 * n : 8 * n + 8]
     arrive("ey", ey_in, far_y)
     fgrad_ref[:, :HALF] = (run[0, rows_of[0]] + ey_in[...].astype(F32)).T.astype(BF16)
     for copy in started:
@@ -585,14 +600,14 @@
             buf(8, HALF, T),
             buf(HALF, T),
             buf(HALF, T),
-            buf(NQ, NZ, 8, HALF, dtype=F32),
-            buf(NQ - 1, NZ, 8, HALF, dtype=F32),
+            buf(NQ, NZ * 8, HALF),
+            buf(NQ - 1, NZ * 8, HALF),
             buf(NZ, 8, HALF, dtype=F32),
             buf(3, NZ, 8, HALF, dtype=F32),
             buf(NZ, 8, HALF, dtype=F32),
             buf(NZ - 1, 8, HALF, dtype=F32),
             buf(NZ, 8, HALF, dtype=F32),
-            buf(NQ, NZ, 8, HALF, dtype=F32),
+            buf(NQ, NZ * 8, HALF),
             pltpu.SemaphoreType.DMA((TILE_PARTS,)),
             pltpu.SemaphoreType.DMA((6,)),
             pltpu.SemaphoreType.DMA((SENDS,)),

time: 93.1 us -> 91.7 us (0.985)
  no operation moved by 1% of the time
where the time goes in v3:
time: 91.7 us; the launch traced here: 91.1 us
  Pallas kernels  88.4 us (96%)
  local copies, waits for them, and re-layouts  2.01 us (2%)
    pallas_call x1, Pallas kernels, local(): pl.pallas_call(kernel, out_shape=(jax.ShapeDtypeStruct((T, T), BF16), jax...  88.4 us
    unnamed x3, local copies, waits for them, and re-layouts  2.01 us

profile of v3, /device:TPU:2, one launch (start us, length us, event | category | flops | bytes accessed | tf_op | source)
XLA Modules:
  0.0 91.1 jit_solution(2098754598417113097)
XLA Ops:
  0.6 88.4 %graph_layer.1 = (bf16[256,256]{1,0:T(8,128)(2,1)S(1)}, bf16[256,256]{1,0:T(8,128)(2,1)S(1)}, f32[256,256]{1,0:T(8,128)S(1)}) custom-call(bf16[256,256]{1,0:T(8,128)(2,1)} %x_hbm.1, bf16[64,256,256]{2,1,0:T(8,128)(2,1)} %tiles_ref.1, s32[1,64]{1,0:T(1,128)} %target_hbm.1, s32[1,32]{1,0:T(1,128)} %count_hbm.1, bf16[256,256]{1,0:T(8,128)(2,1)} %w_hbm.1, ...), custom_call_target="tpu_custom_call" | custom-call | tf_op jit(solution)/shard_map/graph_layer/pallas_call | solution.py:565
  89.0 0.7 copy.12
  89.7 0.7 copy.13
  90.4 0.7 copy.14

commit v4 on v3

--- a/solution.py
+++ b/solution.py
@@ -63,6 +63,10 @@
         )
         copy.start()
         started.append(copy)
+
+    def drain(keep):
+        while len(started) > keep:
+            started.pop(0).wait_send()
 
     def arrive(name, dst, device):
         i = sem_of(name)
@@ -203,10 +207,17 @@
                 far_post(t, tag)
             sib_post(h, t, s, tag)
 
+    def far_step(t):
+        for tag in tags(1, t, 1):
+            arrive(("af", t, tag), piece(1, t, 1, tag, k, split_at(1, t)), far_y)
+            sib_post(1, t, 1, tag)
+
     for t in range(1, FAR + 3):
         if t <= FAR:
             z_step(1, 0, t)
             z_step(0, 0, t)
+        if t == FAR + 1:
+            far_step(FAR)
         if t >= 2:
             sib_wait(t - 2, 1)
             compute(t - 2, 1, 1 - k)
@@ -215,11 +226,7 @@
             compute(t - 1, 0, 1 - k)
         if t <= FAR:
             z_step(0, 1, t)
-        if t - 1 <= FAR:
-            for tag in tags(1, t - 1, 1):
-                arrive(("af", t - 1, tag), piece(1, t - 1, 1, tag, k, split_at(1, t - 1)), far_y)
-                sib_post(1, t - 1, 1, tag)
-        if t <= FAR:
+            far_step(t - 1)
             compute(t, 0, k)
         if t - 1 <= FAR:
             compute(t - 1, 1, k)
@@ -251,6 +258,7 @@
         way = 1 - s
         a_post(2 + 2 * s + way, partial(q_at(way, 1, s), 0), way)
     near_post(3, q_at(0, 0, 0))
+    drain(8)
     for s in range(2):
         arrive(("ba", s), ba_in.at[s], x_next[1 - s])
         a_post(2 + 3 * s, partial(q_at(s, 1, s), 0) + ba_in[s].astype(F32), s)
@@ -329,6 +337,7 @@
             pieces.append(term[up : up + 8, side : side + HALF])
         w_term[q] = jnp.concatenate(pieces, axis=0).astype(BF16)
 
+    drain(8)
     for way in range(2):
         ref = dt.at[dt_at(way, 1, 0), rows_of[0]]
         arrive(("da", 1, 0, way), ref, x_next[1 - way])
@@ -499,6 +508,7 @@
     for_own(3)
     sib_in(3)
     far_sum_post(3)
+    drain(9)
     for_sib(2)
     ring_top(3, 0)
     ring_top(3, 1)
@@ -512,6 +522,7 @@
     ring_top(2, 1)
     sum_group()
     ring_low(3)
+    drain(12)
     for_own(1)
     sib_in(1)
     far_sum_post(1)
@@ -522,6 +533,7 @@
     ring_top(1, 1)
     sib_in(0)
     far_sum_post(0)
+    drain(16)
     ring_low(2)
     spread_rep()
     ring_low(1)
@@ -537,6 +549,7 @@
             post("ey", ey_out, ey_in, far_y)
         else:
             run[0, rows_of[0]] = total
+    drain(12)
     low_total = low_sum(0, 0)
     for way in range(2):
         arrive(("eb", 5 + way), eb_in.at[5 + way], z_next[1 - way])
@@ -551,8 +564,7 @@
             wgrad_ref[up : up + 8, side : side + HALF] = done[8 * n : 8 * n + 8]
     arrive("ey", ey_in, far_y)
     fgrad_ref[:, :HALF] = (run[0, rows_of[0]] + ey_in[...].astype(F32)).T.astype(BF16)
-    for copy in started:
-        copy.wait_send()
+    drain(0)
 
 
 def local(features, tiles, tile_target, tile_count, weight, cotangent):

time: 91.7 us -> 90.8 us (level)
  Pallas kernels: 88.4 us -> 87.3 us
    pallas_call x1, Pallas kernels: 88.4 us -> 87.3 us  [local(): pl.pallas_call(kernel, out_shape=(jax.ShapeDtypeStruct((T, T), BF16), jax...]
where the time goes in v4:
time: 90.8 us; the launch traced here: 90 us
  Pallas kernels  87.3 us (96%)
  local copies, waits for them, and re-layouts  2.01 us (2%)
    pallas_call x1, Pallas kernels, local(): pl.pallas_call(kernel, out_shape=(jax.ShapeDtypeStruct((T, T), BF16), jax...  87.3 us
    unnamed x3, local copies, waits for them, and re-layouts  2.01 us

profile of v4, /device:TPU:2, one launch (start us, length us, event | category | flops | bytes accessed | tf_op | source)
XLA Modules:
  0.0 90.0 jit_solution(8890256365854739336)
XLA Ops:
  0.6 87.3 %graph_layer.1 = (bf16[256,256]{1,0:T(8,128)(2,1)S(1)}, bf16[256,256]{1,0:T(8,128)(2,1)S(1)}, f32[256,256]{1,0:T(8,128)S(1)}) custom-call(bf16[256,256]{1,0:T(8,128)(2,1)} %x_hbm.1, bf16[64,256,256]{2,1,0:T(8,128)(2,1)} %tiles_ref.1, s32[1,64]{1,0:T(1,128)} %target_hbm.1, s32[1,32]{1,0:T(1,128)} %count_hbm.1, bf16[256,256]{1,0:T(8,128)(2,1)} %w_hbm.1, ...), custom_call_target="tpu_custom_call" | custom-call | tf_op jit(solution)/shard_map/graph_layer/pallas_call | solution.py:577
  87.9 0.7 copy.12
  88.6 0.7 copy.13
  89.3 0.7 copy.14

commit v5 on v4

--- a/solution.py
+++ b/solution.py
@@ -216,11 +216,11 @@
         if t <= FAR:
             z_step(1, 0, t)
             z_step(0, 0, t)
-        if t == FAR + 1:
-            far_step(FAR)
         if t >= 2:
             sib_wait(t - 2, 1)
             compute(t - 2, 1, 1 - k)
+        if t == FAR + 1:
+            far_step(FAR)
         if t - 1 <= FAR:
             sib_wait(t - 1, 0)
             compute(t - 1, 0, 1 - k)

time: 90.8 us -> 91.3 us (level)
  no operation moved by 1% of the time
where the time goes in v5:
time: 91.3 us; the launch traced here: 90.5 us
  Pallas kernels  87.8 us (96%)
  local copies, waits for them, and re-layouts  2.01 us (2%)
    pallas_call x1, Pallas kernels, local(): pl.pallas_call(kernel, out_shape=(jax.ShapeDtypeStruct((T, T), BF16), jax...  87.8 us
    unnamed x3, local copies, waits for them, and re-layouts  2.01 us

profile of v5, /device:TPU:2, one launch (start us, length us, event | category | flops | bytes accessed | tf_op | source)
XLA Modules:
  0.0 90.5 jit_solution(12790613516073277559)
XLA Ops:
  0.6 87.8 %graph_layer.1 = (bf16[256,256]{1,0:T(8,128)(2,1)S(1)}, bf16[256,256]{1,0:T(8,128)(2,1)S(1)}, f32[256,256]{1,0:T(8,128)S(1)}) custom-call(bf16[256,256]{1,0:T(8,128)(2,1)} %x_hbm.1, bf16[64,256,256]{2,1,0:T(8,128)(2,1)} %tiles_ref.1, s32[1,64]{1,0:T(1,128)} %target_hbm.1, s32[1,32]{1,0:T(1,128)} %count_hbm.1, bf16[256,256]{1,0:T(8,128)(2,1)} %w_hbm.1, ...), custom_call_target="tpu_custom_call" | custom-call | tf_op jit(solution)/shard_map/graph_layer/pallas_call | solution.py:577
  88.5 0.7 copy.12
  89.1 0.7 copy.13
  89.8 0.7 copy.14
